TPU v7x, 256 devices: a whole 4x4x8 slice. The times are simulated.
256 devices in a mesh: batch: 4 (over x), pool: 32 (over z, y), tensor: 2 (over core).
Axes of the slice: x: 4, y: 4, z: 8, core: 2. Of those that a mesh axis runs over, the one named last changes fastest.
Arguments:
- hidden: bfloat16 [8192, 8192], P(('batch', 'pool'), 'tensor'), may hold values from -6 to 6
- query_base: bfloat16 [8192, 8192], P(('batch', 'pool'), 'tensor'), may hold values from -6 to 6
- new_kv: bfloat16 [8192, 2, 1024], P(('batch', 'pool'), None, 'tensor'), may hold values from -6 to 6
- cache_keys: bfloat16 [8192, 8, 64, 128], P(('batch', 'pool'), 'tensor'), may hold values from -100 to 100
- cache_values: bfloat16 [8192, 8, 64, 128], P(('batch', 'pool'), 'tensor'), may hold values from -6 to 6
- lengths: int32 [8192], P(('batch', 'pool')), may hold values from 1 to 64
- adapter_ids: int32 [2048, 1], P(('batch', 'pool')), may hold values from 0 to 31; in each aligned block of 16 rows (0 to 15, 16 to 31, ...) no two rows name the same one
- adapter_down: bfloat16 [32, 8192, 64], P('pool', 'tensor'), may hold values from -0.0625 to 0.0625
- adapter_up: bfloat16 [32, 64, 8192], P('pool', None, 'tensor'), may hold values from -0.75 to 0.75
Outputs:
- attention: bfloat16 [8192, 8192], P(('batch', 'pool'), 'tensor')
Inputs may be any that keep to these rules, and one draw needn't show every extreme that they name: `adapter_ids`: within the 16 blocks of one device no adapter is named by more than 1 block.
All inputs are finite; a program needn't handle non-finite values.
Results may differ from a plain program's by a relative error of at most 0.011.
Values may be sent and summed in bfloat16 or wider, within the bound.
A program may use at most 128 MiB of HBM per device.

v0:
```python
import math

import jax
import jax.numpy as jnp
from jax import lax
from jax.sharding import PartitionSpec as P

HEAD_SIZE = 128


def attend_scores(query_rows, key_rows):
    return jnp.einsum("rhgd,rhld->rhgl", query_rows, key_rows, preferred_element_type=jnp.float32)


def fresh_scores(query_rows, key_rows):
    return jnp.einsum("rhgd,rhd->rhg", query_rows, key_rows, preferred_element_type=jnp.float32)


def body(
    hidden,
    query_base,
    new_kv,
    cache_keys,
    cache_values,
    lengths,
    adapter_ids,
    adapter_down,
    adapter_up,
):
    row_number, width_local = hidden.shape
    key_value_local = cache_keys.shape[1]
    slot_total = cache_keys.shape[2]
    group_width = width_local // (key_value_local * HEAD_SIZE)
    block_count = adapter_ids.shape[0]
    block_rows = row_number // block_count
    score_scale = 1.0 / math.sqrt(HEAD_SIZE)
    base_query = query_base.reshape(row_number, key_value_local, group_width, HEAD_SIZE)
    new_keys = new_kv[:, 0].reshape(row_number, key_value_local, HEAD_SIZE)
    new_values = new_kv[:, 1].reshape(row_number, key_value_local, HEAD_SIZE)
    base_cached = attend_scores(base_query, cache_keys)
    base_fresh = fresh_scores(base_query, new_keys)
    block_ids = adapter_ids[:, 0]
    row_index_list = jnp.broadcast_to(block_ids[:, None], (block_count, block_rows)).reshape(
        row_number
    )
    fetched = lax.all_gather(adapter_down, "pool", axis=0, tiled=True)
    piece_count = fetched.shape[0]
    chosen = row_index_list[:, None] == jnp.arange(piece_count)[None, :]
    dot_product = jnp.einsum("rd,ndk->rnk", hidden, fetched, preferred_element_type=jnp.float32)
    low_partial = jnp.sum(jnp.where(chosen[:, :, None], dot_product, 0.0), axis=1)
    lowrank = lax.psum(low_partial, "tensor").astype(jnp.bfloat16)
    fetched = lax.all_gather(adapter_up, "pool", axis=0, tiled=True)
    piece_count = fetched.shape[0]
    chosen = row_index_list[:, None] == jnp.arange(piece_count)[None, :]
    masked = jnp.where(chosen[:, :, None], lowrank[:, None, :], jnp.zeros((), jnp.bfloat16))
    adapter_change = jnp.einsum(
        "rnk,nkd->rd", masked, fetched, preferred_element_type=jnp.float32
    ).astype(jnp.bfloat16)
    query_change = adapter_change.reshape(row_number, key_value_local, group_width, HEAD_SIZE)
    cached = (base_cached + attend_scores(query_change, cache_keys)) * score_scale
    fresh = (base_fresh + fresh_scores(query_change, new_keys)) * score_scale
    valid_mask = (jnp.arange(slot_total)[None, :] < lengths[:, None])[:, None, None, :]
    masked_scores = jnp.where(valid_mask, cached, -1e30)
    row_max = jnp.maximum(jnp.max(masked_scores, axis=3), fresh)
    cached_exp = jnp.where(valid_mask, jnp.exp(masked_scores - row_max[..., None]), 0.0)
    fresh_exp = jnp.exp(fresh - row_max)
    row_total = jnp.sum(cached_exp, axis=3) + fresh_exp
    cached_weights = (cached_exp / row_total[..., None]).astype(jnp.bfloat16)
    fresh_weights = (fresh_exp / row_total).astype(jnp.bfloat16)
    mixed = jnp.einsum(
        "rhgl,rhld->rhgd", cached_weights, cache_values, preferred_element_type=jnp.float32
    )
    mixed = (
        mixed
        + fresh_weights.astype(jnp.float32)[..., None]
        * new_values.astype(jnp.float32)[:, :, None, :]
    )
    return mixed.astype(jnp.bfloat16).reshape(row_number, width_local)


def solution(mesh):
    in_specs = (
        P(("batch", "pool"), "tensor"),
        P(("batch", "pool"), "tensor"),
        P(("batch", "pool"), None, "tensor"),
        P(("batch", "pool"), "tensor", None, None),
        P(("batch", "pool"), "tensor", None, None),
        P(("batch", "pool")),
        P(("batch", "pool"), None),
        P("pool", "tensor", None),
        P("pool", None, "tensor"),
    )
    out_specs = P(("batch", "pool"), "tensor")
    return jax.shard_map(body, mesh=mesh, in_specs=in_specs, out_specs=out_specs, check_vma=False)
```

profile of v0, /device:TPU:8, one launch (start us, length us, event | category | flops | bytes accessed | tf_op | source)
XLA Modules:
  0.0 313.5 jit_solution(1261020521034046139)
XLA Ops:
  6.5 0.0 copy-start
  6.5 0.0 all-gather.3.cloned.1.call-start
  6.5 0.7 all-gather.3.cloned.1.call-update
  7.3 0.0 all-gather.5.cloned.1.call-start
  7.3 0.7 all-gather.5.cloned.1.call-update
  8.0 0.7 broadcast_in_dim.69
  8.7 0.1 eq.12
  8.8 1.1 copy.13
  10.0 0.7 iota_compare_fusion
  10.7 1.0 slice_convert_fusion
  11.8 1.3 fusion.18
  13.1 4.4 %fusion.28 = f32[64,4,8,64]{3,2,1,0:T(8,128)S(1)} fusion(bf16[64,4,8,128]{3,2,1,0:T(8,128)(2,1)S(1)} %bitcast.42, bf16[64,4,64,128]{3,2,1,0:T(8,128)(2,1)} %param.12), kind=kOutput, calls=%fused_computation.41 | convolution fusion | flops 33554432 | bytes 5242880 | tf_op jit(solution)/shard_map/rhgd,rhld->rhgl/dot_general | solution.py:12
  17.5 134.7 %all-gather.3.cloned.1.call-done = bf16[32,4096,64]{1,2,0:T(8,128)(2,1)} async-done(((bf16[1,4096,64]{1,2,0:T(8,128)(2,1)}), bf16[32,4096,64]{1,2,0:T(8,128)(2,1)}) %all-gather.3.cloned.1.call-update) | async-done | bytes 16777232 | tf_op jit(solution)/shard_map/all_gather | solution.py:46
  152.2 0.0 copy-done
  152.2 13.8 %fusion.4 = f32[64,64]{1,0:T(8,128)S(1)} fusion(bf16[32,4096,64]{1,2,0:T(8,128)(2,1)} %all-gather.3.cloned.1.call-done, bf16[64,4096]{1,0:T(8,128)(2,1)S(1)} %copy-done, pred[64,32]{0,1:T(8,128)(4,1)S(1)} %iota_compare_fusion.1), kind=kOutput, calls=%fused_computation.8 | convolution fusion | flops 1073999872 | bytes 17319936 | tf_op jit(solution)/shard_map/rd,ndk->rnk/dot_general | solution.py:49
  166.0 3.6 %psum.7 = bf16[64,64]{1,0:T(8,128)(2,1)S(1)} all-reduce(f32[64,64]{1,0:T(8,128)S(1)} %fusion.4), channel_id=1, replica_groups=mesh['batch'=4,'pool'=32,'tensor'=2] {'tensor'}, use_global_device_ids=true, to_apply=%region_1.2 | all-reduce | flops 4096 | bytes 24576 | tf_op jit(solution)/shard_map/psum | solution.py:51
  169.6 0.0 copy-start.2
  169.6 122.8 %all-gather.5.cloned.1.call-done = bf16[32,64,4096]{2,1,0:T(8,128)(2,1)} async-done(((bf16[1,64,4096]{2,1,0:T(8,128)(2,1)}), bf16[32,64,4096]{2,1,0:T(8,128)(2,1)}) %all-gather.5.cloned.1.call-update) | async-done | bytes 16777232 | tf_op jit(solution)/shard_map/all_gather | solution.py:52
  292.5 0.0 copy-start.1
  292.5 7.7 %fusion.5 = bf16[8,8,32,128]{3,1,2,0:T(8,128)(2,1)S(1)} fusion(bf16[32,64,4096]{2,1,0:T(8,128)(2,1)} %all-gather.5.cloned.1.call-done, pred[64,32]{0,1:T(8,128)(4,1)S(1)} %iota_compare_fusion.1, bf16[64,64]{1,0:T(8,128)(2,1)S(1)} %psum.7), kind=kOutput, calls=%fused_computation.9 | convolution fusion | flops 1074135040 | bytes 17311744 | tf_op jit(solution)/shard_map/rnk,nkd->rd/dot_general | solution.py:56
  300.2 0.1 copy.14
  300.3 0.0 copy-done.2
  300.3 0.4 fusion.16
  300.7 0.0 copy-done.1
  300.7 0.0 copy-start.3
  300.7 2.5 fusion.27
  303.2 0.1 fusion.23
  303.3 0.8 fusion.6
  304.0 0.1 fusion.26
  304.1 0.0 copy-done.3
  304.2 1.5 fusion.3
  305.7 1.0 copy.17
  (1 shorter events, 0.0 us)
Async XLA Ops:
  6.5 145.7 %copy-start = (bf16[64,4096]{1,0:T(8,128)(2,1)S(1)}, bf16[64,4096]{1,0:T(8,128)(2,1)}, u32[]{:S(2)}) copy-start(bf16[64,4096]{1,0:T(8,128)(2,1)} %param.9) | copy-start | bytes 1572868
  6.5 145.7 %all-gather.3.cloned.1.call-start = ((), (), s32[]{:S(2)}) async-start(), calls=%async_computation | async-start | bytes 17301504 | tf_op jit(solution)/shard_map/all_gather | solution.py:46
  7.3 285.2 %all-gather.5.cloned.1.call-start = ((), (), s32[]{:S(2)}) async-start(), calls=%async_computation.1 | async-start | bytes 17301504 | tf_op jit(solution)/shard_map/all_gather | solution.py:52
  169.6 130.7 %copy-start.2 = (bf16[64,2,512]{2,1,0:T(2,128)(2,1)S(1)}, bf16[64,2,512]{2,1,0:T(2,128)(2,1)}, u32[]{:S(2)}) copy-start(bf16[64,2,512]{2,1,0:T(2,128)(2,1)} %param.11) | copy-start | bytes 393220
  292.5 8.2 %copy-start.1 = (bf16[64,4,64,128]{3,2,1,0:T(8,128)(2,1)S(1)}, bf16[64,4,64,128]{3,2,1,0:T(8,128)(2,1)}, u32[]{:S(2)}) copy-start(bf16[64,4,64,128]{3,2,1,0:T(8,128)(2,1)} %param.12) | copy-start | bytes 12582916
  300.7 3.4 %copy-start.3 = (bf16[64,4,64,128]{3,2,1,0:T(8,128)(2,1)S(1)}, bf16[64,4,64,128]{3,2,1,0:T(8,128)(2,1)}, u32[]{:S(2)}) copy-start(bf16[64,4,64,128]{3,2,1,0:T(8,128)(2,1)} %param.13) | copy-start | bytes 12582916
Sparse Core Ops, SparseCore 0:
  9.9 142.2 all-gather.2
  154.8 137.6 all-gather.4
where the time goes:
time: 316 us; the launch traced here: 314 us
  waiting for transfers between devices  259 us (82%)
  matrix products  31.7 us (10%)
  between operations  13.5 us (4%)
  blocking collectives  3.58 us (1%)
    all_gather x1, waiting for transfers between devices, body(): fetched = lax.all_gather(adapter_down, 'pool', axis=0, tiled=True)  135 us
    all_gather x1, waiting for transfers between devices, body(): fetched = lax.all_gather(adapter_up, 'pool', axis=0, tiled=True)  123 us
    dot_general x1, matrix products, body(): jnp.einsum('rd,ndk->rnk', hidden, fetched, preferred_element_type=jnp.flo...  13.8 us
    dot_general x1, matrix products, body(): jnp.einsum('rnk,nkd->rd', masked, fetched, preferred_element_type=jnp.flo...  7.7 us
    dot_general x2, matrix products, attend_scores(): jnp.einsum('rhgd,rhld->rhgl', query_rows, key_rows, preferred_element_typ...  6.89 us
  transfers between devices with their start and end apart: 2, of which 2 were waited for; matrix products, arithmetic and copies ran while one was open for 7% of the time, Pallas kernels for 0%

commit v1 on v0

v1 whole, which is shorter than its diff:
```python
import functools
import math

import jax
import jax.numpy as jnp
from jax import lax
from jax.experimental import pallas as pl
from jax.experimental.pallas import tpu as pltpu
from jax.sharding import PartitionSpec as P

HEAD_SIZE = 128
CHIPS_Y = 4
LANES = 128
MESH = pl.DeviceIdType.MESH
NT = (((1,), (1,)), ((), ()))
NN = (((1,), (0,)), ((), ()))
VMEM_LIMIT = 56 * 1024 * 1024


def wait_bytes(ref, sem):
    pltpu.make_async_copy(ref, ref, sem).wait()


def delta_kernel(
    sizes,
    ids_ref,
    hidden_ref,
    down_ref,
    up_ref,
    out_ref,
    rows_in,
    ids_own,
    ids_in,
    downs,
    ups,
    picked,
    key_rows,
    odd_rows,
    partial,
    partial_in,
    low_own,
    low_in,
    delta,
    local_sem,
    rows_send,
    rows_recv,
    ids_send,
    ids_recv,
    slice_send,
    ring_send,
    ring_recv,
    partial_send,
    partial_recv,
    low_send,
    low_recv,
    delta_send,
    delta_recv,
):
    nx, ny, nz, nt = sizes
    plane = nx * ny
    team = plane * nt
    rows, width = hidden_ref.shape
    rank = down_ref.shape[0]
    part = width // plane
    total_rows = plane * rows
    half_rows = total_rows // 2
    blocks = ids_ref.shape[0]
    block_rows = rows // blocks
    pack = half_rows // team

    x = lax.axis_index("batch")
    pool = lax.axis_index("pool")
    t = lax.axis_index("tensor")
    z = pool // ny
    y = pool % ny
    slot = x * ny + y
    seat = slot * nt + t

    def at_slot(s):
        return (s // ny, z * ny + s % ny, t)

    def at_seat(q):
        return (q // (ny * nt), z * ny + (q // nt) % ny, q % nt)

    def at_z(zz):
        return (x, zz * ny + y, t)

    def columns(s):
        return pl.ds(pl.multiple_of(s * part, part), part)

    barrier = pltpu.get_barrier_semaphore()

    def greet(i, carry):
        pl.semaphore_signal(barrier, 1, device_id=at_seat((seat + i) % team), device_id_type=MESH)
        return carry

    lax.fori_loop(1, team, greet, 0)
    pl.semaphore_signal(barrier, 1, device_id=at_z((z + 1) % nz), device_id_type=MESH)
    pl.semaphore_signal(barrier, 1, device_id=at_z((z + nz - 1) % nz), device_id_type=MESH)

    block_iota = lax.broadcasted_iota(jnp.int32, (blocks, LANES), 0)
    named = jnp.zeros((blocks, LANES), jnp.int32)
    for b in range(blocks):
        named = jnp.where(block_iota == b, ids_ref[b], named)
    ids_own[...] = named.astype(jnp.float32).astype(jnp.bfloat16)
    ids_in[slot] = ids_own[...]

    own_rows = pltpu.make_async_copy(hidden_ref.at[:, columns(slot)], rows_in.at[slot], local_sem.at[0])
    own_rows.start()
    own_down = pltpu.make_async_copy(down_ref.at[:, columns(slot)], downs.at[z, y], local_sem.at[1])
    own_down.start()
    own_up = pltpu.make_async_copy(up_ref.at[:, columns(slot)], ups.at[z, y], local_sem.at[2])
    own_up.start()

    pl.semaphore_wait(barrier, team + 1)

    def ring_copy(kind, buffer, zz, yy, to, side):
        if side < 2:
            ref = buffer.at[zz, yy]
        else:
            ref = buffer.at[zz, yy, pl.ds((side - 2) * (rank // 2), rank // 2)]
        return pltpu.make_async_remote_copy(
            src_ref=ref,
            dst_ref=ref,
            send_sem=ring_send.at[kind],
            recv_sem=ring_recv.at[kind, zz, yy, max(side - 2, 0)],
            device_id=at_z(to),
            device_id_type=MESH,
        )

    right, left = (z + 1) % nz, (z + nz - 1) % nz
    full = nz // 2 - 1

    def slice_exchange(kind, source, buffer):
        def send(i, carry):
            yy = (y + i) % ny
            pltpu.make_async_remote_copy(
                src_ref=source.at[:, columns(x * ny + yy)],
                dst_ref=buffer.at[z, y],
                send_sem=slice_send.at[kind],
                recv_sem=ring_recv.at[kind, z, y, 0],
                device_id=(x, z * ny + yy, t),
                device_id_type=MESH,
            ).start()
            return carry

        lax.fori_loop(1, ny, send, 0)

    def ring_first(kind, buffer):
        def one(i, carry):
            yy = (y + i) % ny

            @pl.when(i > 0)
            def _():
                wait_bytes(buffer.at[z, yy], ring_recv.at[kind, z, yy, 0])

            ring_copy(kind, buffer, z, yy, right, 0).start()
            ring_copy(kind, buffer, z, yy, left, 1).start()
            return carry

        lax.fori_loop(0, ny, one, 0)

    def ring_step(kind, buffer, k):
        def one(i, carry):
            yy = (y + i) % ny
            for side, zz, to in ((0, (z + nz - k) % nz, right), (1, (z + k) % nz, left)):
                if k <= full:
                    wait_bytes(buffer.at[zz, yy], ring_recv.at[kind, zz, yy, 0])
                    ring_copy(kind, buffer, zz, yy, to, side if k < full else side + 2).start()
                else:
                    wait_bytes(
                        buffer.at[zz, yy, pl.ds(side * (rank // 2), rank // 2)],
                        ring_recv.at[kind, zz, yy, side],
                    )
            return carry

        lax.fori_loop(0, ny, one, 0)

    slice_exchange(0, down_ref, downs)

    def send_rows(i, carry):
        s = (slot + i) % plane
        pltpu.make_async_remote_copy(
            src_ref=ids_own,
            dst_ref=ids_in.at[slot],
            send_sem=ids_send,
            recv_sem=ids_recv,
            device_id=at_slot(s),
            device_id_type=MESH,
        ).start()
        pltpu.make_async_remote_copy(
            src_ref=hidden_ref.at[:, columns(s)],
            dst_ref=rows_in.at[slot],
            send_sem=rows_send,
            recv_sem=rows_recv,
            device_id=at_slot(s),
            device_id_type=MESH,
        ).start()
        return carry

    lax.fori_loop(1, plane, send_rows, 0)
    own_down.wait()
    ring_first(0, downs)
    slice_exchange(1, up_ref, ups)

    wait_bytes(ids_in.at[pl.ds(0, plane - 1)], ids_recv)
    spread = lax.broadcasted_iota(jnp.int32, (rows, blocks), 0) // block_rows == lax.broadcasted_iota(
        jnp.int32, (rows, blocks), 1
    )
    spread = jnp.where(spread, 1.0, 0.0).astype(jnp.bfloat16)

    def expand(s, carry):
        ids = lax.dot_general(spread, ids_in[s], NN, preferred_element_type=jnp.float32).astype(jnp.int32)
        at = pl.ds(pl.multiple_of(s * rows, rows), rows)
        key_rows[at, :] = ids // 2
        odd_rows[at, :] = ids % 2
        return carry

    lax.fori_loop(0, plane, expand, 0)

    own_rows.wait()
    wait_bytes(rows_in.at[pl.ds(0, plane - 1)], rows_recv)

    def use_down(zz, first):
        weights = downs[zz].reshape(ny * rank, part)

        def one(i, carry):
            lhs = rows_in[pl.ds(2 * i, 2)].reshape(2 * rows, part)
            product = lax.dot_general(lhs, weights, NT, preferred_element_type=jnp.float32)
            at = pl.ds(pl.multiple_of(i * 2 * rows, 2 * rows), 2 * rows)
            keys = key_rows[at, :]
            value = jnp.zeros((2 * rows, LANES), jnp.float32) if first else picked[at, :]
            for g in range(ny * rank // LANES):
                value = jnp.where(
                    keys == zz * (ny * rank // LANES) + g, product[:, g * LANES : (g + 1) * LANES], value
                )
            picked[at, :] = value
            return carry

        lax.fori_loop(0, plane // 2, one, 0)

    use_down(z, True)
    for k in range(1, full + 1):
        ring_step(0, downs, k)
        use_down((z + nz - k) % nz, False)
        use_down((z + k) % nz, False)
    own_up.wait()
    ring_first(1, ups)
    ring_step(0, downs, full + 1)
    use_down((z + full + 1) % nz, False)

    def fold(s, carry):
        both = []
        upper = lax.broadcasted_iota(jnp.int32, (rows, LANES), 1) // rank
        for h in range(2):
            at = pl.ds(pl.multiple_of(h * half_rows + s * rows, rows), rows)
            kept = jnp.where(odd_rows[at, :] == upper, picked[at, :], 0.0)
            both.append(kept + pltpu.roll(kept, rank, 1))
        partial[pl.ds(pl.multiple_of(s * rows, rows), rows), :] = jnp.where(upper == 0, both[0], both[1])
        return carry

    lax.fori_loop(0, plane // 2, fold, 0)

    def packed(q):
        return pl.ds(pl.multiple_of(q * pack, pack), pack)

    def send_partial(i, carry):
        q = (seat + i) % team
        pltpu.make_async_remote_copy(
            src_ref=partial.at[packed(q)],
            dst_ref=partial_in.at[seat],
            send_sem=partial_send,
            recv_sem=partial_recv,
            device_id=at_seat(q),
            device_id_type=MESH,
        ).start()
        return carry

    lax.fori_loop(1, team, send_partial, 0)
    partial_in[seat] = partial[packed(seat), :]
    ring_step(1, ups, 1)
    wait_bytes(partial_in.at[pl.ds(0, team - 1)], partial_recv)
    low = jnp.sum(partial_in[...], axis=0).astype(jnp.bfloat16)
    low_own[...] = low
    low_in[seat] = low

    def send_low(i, carry):
        pltpu.make_async_remote_copy(
            src_ref=low_own,
            dst_ref=low_in.at[seat],
            send_sem=low_send,
            recv_sem=low_recv,
            device_id=at_seat((seat + i) % team),
            device_id_type=MESH,
        ).start()
        return carry

    lax.fori_loop(1, team, send_low, 0)
    for k in range(2, full + 2):
        ring_step(1, ups, k)
    wait_bytes(low_in.at[pl.ds(0, team - 1)], low_recv)

    groups = nz * ny * rank // LANES

    def use_up(i, carry):
        p = (slot + i) % (plane // 2)
        per = rows // pack
        low = low_in[pl.ds(p * per, per)].reshape(rows, LANES).astype(jnp.float32)
        turned = pltpu.roll(low, rank, 1)
        upper = lax.broadcasted_iota(jnp.int32, (rows, LANES), 1) // rank
        doubled = (jnp.where(upper == 0, low, turned), jnp.where(upper == 0, turned, low))
        lhs = []
        for h in range(2):
            at = pl.ds(pl.multiple_of(h * half_rows + p * rows, rows), rows)
            kept = jnp.where(odd_rows[at, :] == upper, doubled[h], 0.0)
            keys = key_rows[at, :]
            lhs.append(
                jnp.concatenate([jnp.where(keys == g, kept, 0.0).astype(jnp.bfloat16) for g in range(groups)], axis=1)
            )
        lhs = jnp.concatenate(lhs, axis=0)
        result = lax.dot_general(
            lhs, ups[...].reshape(nz * ny * rank, part), NN, preferred_element_type=jnp.float32
        ).astype(jnp.bfloat16)
        for h in range(2):
            s = p + h * (plane // 2)
            delta[s] = result[h * rows : (h + 1) * rows]

            @pl.when(s == slot)
            def _():
                pltpu.make_async_copy(delta.at[s], out_ref.at[:, columns(slot)], local_sem.at[3]).start()

            @pl.when(s != slot)
            def _():
                pltpu.make_async_remote_copy(
                    src_ref=delta.at[s],
                    dst_ref=out_ref.at[:, columns(slot)],
                    send_sem=delta_send,
                    recv_sem=delta_recv,
                    device_id=at_slot(s),
                    device_id_type=MESH,
                ).start()

        return carry

    lax.fori_loop(0, plane // 2, use_up, 0)

    wait_bytes(delta.at[0], local_sem.at[3])
    wait_bytes(delta.at[pl.ds(0, plane - 1)], delta_recv)
    wait_bytes(delta.at[pl.ds(0, plane - 1)], delta_send)
    wait_bytes(rows_in.at[pl.ds(0, plane - 1)], rows_send)
    wait_bytes(ids_in.at[pl.ds(0, plane - 1)], ids_send)
    wait_bytes(partial_in.at[pl.ds(0, team - 1)], partial_send)
    wait_bytes(low_in.at[pl.ds(0, team - 1)], low_send)
    for kind, buffer in ((0, downs), (1, ups)):
        wait_bytes(buffer.at[0, pl.ds(0, ny - 1)], slice_send.at[kind])
        wait_bytes(buffer.at[pl.ds(0, 2 * full + 1)], ring_send.at[kind])


def adapter_delta(ids, hidden, down, up, sizes):
    nx, ny, nz, nt = sizes
    plane = nx * ny
    team = plane * nt
    rows, width = hidden.shape
    rank = down.shape[0]
    part = width // plane
    blocks = ids.shape[0]
    total = plane * rows
    pack = total // 2 // team
    bf16, f32, i32 = jnp.bfloat16, jnp.float32, jnp.int32
    dma = pltpu.SemaphoreType.DMA
    anywhere = pl.BlockSpec(memory_space=pl.ANY)
    return pl.pallas_call(
        functools.partial(delta_kernel, sizes),
        out_shape=jax.ShapeDtypeStruct((rows, width), bf16),
        in_specs=[pl.BlockSpec(memory_space=pltpu.SMEM), anywhere, anywhere, anywhere],
        out_specs=anywhere,
        scratch_shapes=[
            pltpu.VMEM((plane, rows, part), bf16),
            pltpu.VMEM((blocks, LANES), bf16),
            pltpu.VMEM((plane, blocks, LANES), bf16),
            pltpu.VMEM((nz, ny, rank, part), bf16),
            pltpu.VMEM((nz, ny, rank, part), bf16),
            pltpu.VMEM((total, LANES), f32),
            pltpu.VMEM((total, LANES), i32),
            pltpu.VMEM((total, LANES), i32),
            pltpu.VMEM((total // 2, LANES), f32),
            pltpu.VMEM((team, pack, LANES), f32),
            pltpu.VMEM((pack, LANES), bf16),
            pltpu.VMEM((team, pack, LANES), bf16),
            pltpu.VMEM((plane, rows, part), bf16),
            dma((4,)),
            dma,
            dma,
            dma,
            dma,
            dma((2,)),
            dma((2,)),
            dma((2, nz, ny, 2)),
            dma,
            dma,
            dma,
            dma,
            dma,
            dma,
        ],
        compiler_params=pltpu.CompilerParams(
            collective_id=0, has_side_effects=True, vmem_limit_bytes=VMEM_LIMIT
        ),
    )(ids, hidden, down, up)


def attend_kernel(lengths_ref, base_ref, delta_ref, fresh_ref, keys_ref, values_ref, out_ref):
    step = pl.program_id(0)
    rows = base_ref.shape[0]
    heads = keys_ref.shape[1]
    slots = keys_ref.shape[2]
    group = base_ref.shape[1] // (heads * HEAD_SIZE)
    eight = 8
    scale = 1.0 / math.sqrt(HEAD_SIZE)
    tall = group * eight
    request = lax.broadcasted_iota(jnp.int32, (tall, LANES), 0) % eight
    lane = lax.broadcasted_iota(jnp.int32, (tall, LANES), 1)
    pair = request // 2
    mine = lane // slots == request % 2
    place = lane % slots
    fresh_lane = jnp.logical_and(jnp.logical_not(mine), place == request)
    limits = []
    for u in range(rows // eight):
        limit = jnp.zeros((tall, LANES), jnp.int32)
        for i in range(eight):
            limit = jnp.where(request == i, lengths_ref[step * rows + u * eight + i], limit)
        limits.append(limit)
    blank = jnp.zeros((slots - eight, HEAD_SIZE), jnp.bfloat16)

    def stack(ref, u, h):
        wide = ref[:, h * group * HEAD_SIZE : (h + 1) * group * HEAD_SIZE].astype(jnp.float32)
        wide = wide[u * eight : (u + 1) * eight]
        return jnp.concatenate([wide[:, g * HEAD_SIZE : (g + 1) * HEAD_SIZE] for g in range(group)], axis=0)

    for h in range(heads):
        outs = []
        for u in range(rows // eight):
            queries = jnp.concatenate([stack(base_ref, u, h), stack(delta_ref, u, h)], axis=0).astype(jnp.bfloat16)
            of = slice(u * eight, (u + 1) * eight)
            new = []
            for i in range(2):
                first = (i * heads + h) * HEAD_SIZE
                rows_new = fresh_ref[:, first : first + HEAD_SIZE].astype(jnp.float32)[of].astype(jnp.bfloat16)
                new.append(jnp.concatenate([rows_new, blank, rows_new, blank], axis=0))
            keys = jnp.concatenate([keys_ref[of, h].reshape(eight * slots, HEAD_SIZE), new[0]], axis=0)
            values = jnp.concatenate([values_ref[of, h].reshape(eight * slots, HEAD_SIZE), new[1]], axis=0)
            scores = lax.dot_general(queries, keys, NT, preferred_element_type=jnp.float32)
            scores = (scores[:tall] + scores[tall:]) * scale
            chosen = scores[:, :LANES]
            for j in range(1, eight // 2):
                chosen = jnp.where(pair == j, scores[:, j * LANES : (j + 1) * LANES], chosen)
            valid = jnp.logical_and(mine, place < limits[u])
            chosen = jnp.where(valid, chosen, jnp.where(fresh_lane, scores[:, -LANES:], -1e30))
            top = jnp.max(chosen, axis=1, keepdims=True)
            raised = jnp.where(jnp.logical_or(valid, fresh_lane), jnp.exp(chosen - top), 0.0)
            weights = raised / jnp.sum(raised, axis=1, keepdims=True)
            cached = jnp.where(mine, weights, 0.0)
            parts = [jnp.where(pair == j, cached, 0.0) for j in range(eight // 2)]
            parts.append(jnp.where(mine, 0.0, weights))
            spread = jnp.concatenate(parts, axis=1).astype(jnp.bfloat16)
            outs.append(lax.dot_general(spread, values, NN, preferred_element_type=jnp.float32))
        for g in range(group):
            first = (h * group + g) * HEAD_SIZE
            block = jnp.concatenate([o[g * eight : (g + 1) * eight] for o in outs], axis=0)
            out_ref[:, first : first + HEAD_SIZE] = block.astype(jnp.bfloat16)


def attend(lengths, base, delta, fresh, keys, values):
    rows, width = base.shape
    heads, slots = keys.shape[1:3]
    step = 16
    cache = pl.BlockSpec((step, heads, slots, HEAD_SIZE), lambda i: (i, 0, 0, 0))
    flat = pl.BlockSpec((step, width), lambda i: (i, 0))
    return pl.pallas_call(
        attend_kernel,
        grid=(rows // step,),
        out_shape=jax.ShapeDtypeStruct((rows, width), jnp.bfloat16),
        in_specs=[
            pl.BlockSpec(memory_space=pltpu.SMEM),
            flat,
            flat,
            pl.BlockSpec((step, fresh.shape[1]), lambda i: (i, 0)),
            cache,
            cache,
        ],
        out_specs=flat,
        compiler_params=pltpu.CompilerParams(vmem_limit_bytes=VMEM_LIMIT),
    )(lengths, base, delta, fresh, keys, values)


def body(
    sizes,
    hidden,
    query_base,
    new_kv,
    cache_keys,
    cache_values,
    lengths,
    adapter_ids,
    adapter_down,
    adapter_up,
):
    down = jnp.swapaxes(adapter_down, 1, 2)[0]
    delta = adapter_delta(adapter_ids[:, 0], hidden, down, adapter_up[0], sizes)
    fresh = new_kv.reshape(new_kv.shape[0], -1)
    return attend(lengths, query_base, delta, fresh, cache_keys, cache_values)


def solution(mesh):
    in_specs = (
        P(("batch", "pool"), "tensor"),
        P(("batch", "pool"), "tensor"),
        P(("batch", "pool"), None, "tensor"),
        P(("batch", "pool"), "tensor", None, None),
        P(("batch", "pool"), "tensor", None, None),
        P(("batch", "pool")),
        P(("batch", "pool"), None),
        P("pool", "tensor", None),
        P("pool", None, "tensor"),
    )
    out_specs = P(("batch", "pool"), "tensor")
    pool = mesh.shape["pool"]
    sizes = (mesh.shape["batch"], CHIPS_Y, pool // CHIPS_Y, mesh.shape["tensor"])
    return jax.shard_map(
        functools.partial(body, sizes), mesh=mesh, in_specs=in_specs, out_specs=out_specs, check_vma=False
    )
```

time: 316 us -> 81.9 us (0.26)
  waiting for transfers between devices: 259 us -> 0 us
  Pallas kernels: 0 us -> 79.4 us
  matrix products: 31.7 us -> 0 us
  between operations: 13.5 us -> 0.01 us
  blocking collectives: 3.58 us -> 0 us
    all_gather x2 -> x0, waiting for transfers between devices: 258 us -> none  [the longest x1 135 us: body(): fetched = lax.all_gather(adapter_down, 'pool', axis=0, tiled=True)]
    pallas_call x0 -> x2, Pallas kernels: none -> 79.4 us  [the longest x1 64.2 us: adapter_delta(): pl.pallas_call(functools.partial(delta_kernel, sizes), out_shape=jax.Shap...]
    dot_general x7 -> x0, matrix products: 31.7 us -> none  [the longest x1 13.8 us: body(): jnp.einsum('rd,ndk->rnk', hidden, fetched, preferred_element_type=jnp.flo...]
    psum x1 -> x0, blocking collectives: 3.58 us -> none  [body(): lowrank = lax.psum(low_partial, 'tensor').astype(jnp.bfloat16)]
  transfers between devices with their start and end apart: 2 -> 0, of which waited for: 2 -> 0; matrix products, arithmetic and copies ran while one was open for 7% -> 0% of each run, Pallas kernels for 0% -> 0%
where the time goes in v1:
time: 81.9 us; the launch traced here: 80.9 us
  Pallas kernels  79.4 us (97%)
  local copies, waits for them, and re-layouts  1.57 us (2%)
    pallas_call x1, Pallas kernels, adapter_delta(): pl.pallas_call(functools.partial(delta_kernel, sizes), out_shape=jax.Shap...  64.2 us
    pallas_call x1, Pallas kernels, attend(): pl.pallas_call(attend_kernel, grid=(rows // step,), out_shape=jax.ShapeDt...  15.2 us

profile of v1, /device:TPU:8, one launch (start us, length us, event | category | flops | bytes accessed | tf_op | source)
XLA Modules:
  0.0 80.9 jit_solution(2136161308511120883)
XLA Ops:
  0.0 1.6 %copy.10 = bf16[8,8,2,512]{3,1,2,0:T(8,128)(2,1)} copy(bf16[8,8,2,512]{3,2,1,0:T(2,128)(2,1)} %bitcast.10) | data formatting | bytes 262144
  1.6 64.2 %shard_map.91.delta_ref = bf16[64,4096]{1,0:T(8,128)(2,1)} custom-call(s32[16]{0:T(128)} %bitcast.11, bf16[64,4096]{1,0:T(8,128)(2,1)} %hidden_ref.1, bf16[64,4096]{1,0:T(8,128)(2,1)} %bitcast.8, bf16[64,4096]{1,0:T(8,128)(2,1)} %bitcast.9), custom_call_target="tpu_custom_call" | custom-call | tf_op jit(solution)/shard_map/pallas_call | solution.py:372
  65.7 15.2 %shard_map.92 = bf16[64,4096]{1,0:T(8,128)(2,1)} custom-call(s32[64]{0:T(128)} %lengths_ref.1, bf16[64,4096]{1,0:T(8,128)(2,1)} %base_ref.1, bf16[64,4096]{1,0:T(8,128)(2,1)} %shard_map.91.delta_ref, bf16[64,1024]{1,0:T(8,128)(2,1)} %bitcast.7, bf16[64,4,64,128]{3,2,1,0:T(8,128)(2,1)} %keys_ref.1, bf16[64,4,64,128]{3,2,1,0:T(8,128)(2,1)} %values_ref.1), custom_call_target="tpu_custom_call" | custom-call | tf_op jit(solution)/shard_map/pallas_call | solution.py:479

commit v2 on v1

v2 whole, which is shorter than its diff:
```python
import functools
import math

import jax
import jax.numpy as jnp
from jax import lax
from jax.experimental import pallas as pl
from jax.experimental.pallas import tpu as pltpu
from jax.sharding import PartitionSpec as P

HEAD_SIZE = 128
CHIPS_Y = 4
LANES = 128
EIGHT = 8
MESH = pl.DeviceIdType.MESH
NT = (((1,), (1,)), ((), ()))
NN = (((1,), (0,)), ((), ()))
VMEM_LIMIT = 56 * 1024 * 1024


def wait_bytes(ref, sem):
    pltpu.make_async_copy(ref, ref, sem).wait()


def kernel(
    sizes,
    ids_ref,
    lengths_ref,
    hidden_ref,
    base_ref,
    fresh_ref,
    keys_ref,
    values_ref,
    down_ref,
    up_ref,
    out_ref,
    rows_in,
    ids_own,
    ids_in,
    downs,
    ups,
    picked,
    key_rows,
    odd_rows,
    partial,
    partner_in,
    reduced,
    partial_in,
    low_own,
    low_in,
    delta,
    delta_in,
    queries,
    fresh,
    new_keys,
    new_values,
    keys,
    values,
    scores_base,
    result,
    local_sem,
    out_sem,
    rows_send,
    rows_recv,
    ids_send,
    ids_recv,
    slice_send,
    ring_send,
    ring_recv,
    partner_send,
    partner_recv,
    partial_send,
    partial_recv,
    low_send,
    low_recv,
    delta_send,
    delta_recv,
):
    nx, ny, nz, nt = sizes
    plane = nx * ny
    team = plane * nt
    rows, width = hidden_ref.shape
    rank = down_ref.shape[0]
    part = width // plane
    half_rows = plane * rows // 2
    blocks = ids_ref.shape[0]
    block_rows = rows // blocks
    pack = half_rows // team
    heads, slots = keys_ref.shape[1:3]
    group = width // (heads * HEAD_SIZE)
    tall = group * EIGHT
    scale = 1.0 / math.sqrt(HEAD_SIZE)
    assert heads == nx and ny * part == group * HEAD_SIZE

    x = lax.axis_index("batch")
    pool = lax.axis_index("pool")
    t = lax.axis_index("tensor")
    z = pool // ny
    y = pool % ny
    slot = x * ny + y
    seat = t * plane + slot

    def columns(s):
        return pl.ds(pl.multiple_of(s * part, part), part)

    def peer(i):
        return (x + nx // 2 + i // ny) % nx, (y + ny // 2 + i) % ny

    myself = (nx - nx // 2) % nx * ny + (ny - ny // 2) % ny

    def each_peer(one):
        lax.fori_loop(0, myself, one, 0)
        lax.fori_loop(myself + 1, plane, one, 0)

    right, left = (z + 1) % nz, (z + nz - 1) % nz
    full = nz // 2 - 1

    barrier = pltpu.get_barrier_semaphore()

    def greet(i, carry):
        px, py = peer(i)
        for pt in range(nt):
            pl.semaphore_signal(barrier, 1, device_id=(px, z * ny + py, pt), device_id_type=MESH)
        return carry

    each_peer(greet)
    for other in range(1, nt):
        pl.semaphore_signal(barrier, 1, device_id=(x, pool, (t + other) % nt), device_id_type=MESH)
    for zz in (right, left):
        pl.semaphore_signal(barrier, 1, device_id=(x, zz * ny + y, t), device_id_type=MESH)

    local = [
        pltpu.make_async_copy(hidden_ref.at[:, columns(slot)], rows_in.at[slot], local_sem.at[0]),
        pltpu.make_async_copy(down_ref.at[:, columns(slot)], downs.at[z, y], local_sem.at[1]),
        pltpu.make_async_copy(up_ref.at[:, columns(slot)], ups.at[z, y], local_sem.at[2]),
        pltpu.make_async_copy(base_ref, queries, local_sem.at[3]),
        pltpu.make_async_copy(fresh_ref, fresh, local_sem.at[4]),
        pltpu.make_async_copy(keys_ref, keys, local_sem.at[5]),
        pltpu.make_async_copy(values_ref, values, local_sem.at[6]),
    ]
    for copy in (local[1], local[0], local[2]):
        copy.start()

    block_iota = lax.broadcasted_iota(jnp.int32, (blocks, LANES), 0)
    named = jnp.zeros((blocks, LANES), jnp.int32)
    for b in range(blocks):
        named = jnp.where(block_iota == b, ids_ref[b], named)
    ids_own[...] = named.astype(jnp.float32).astype(jnp.bfloat16)
    ids_in[slot] = ids_own[...]

    pl.semaphore_wait(barrier, team + 1)

    def slice_exchange(kind, source, buffer):
        def send(i, carry):
            yy = (y + i) % ny
            pltpu.make_async_remote_copy(
                src_ref=source.at[:, columns(x * ny + yy)],
                dst_ref=buffer.at[z, y],
                send_sem=slice_send.at[kind],
                recv_sem=ring_recv.at[kind, z, y, 0],
                device_id=(x, z * ny + yy, t),
                device_id_type=MESH,
            ).start()
            return carry

        lax.fori_loop(1, ny, send, 0)

    def ring_copy(kind, buffer, zz, yy, to, side):
        if side < 2:
            ref = buffer.at[zz, yy]
        else:
            ref = buffer.at[zz, yy, pl.ds((side - 2) * (rank // 2), rank // 2)]
        return pltpu.make_async_remote_copy(
            src_ref=ref,
            dst_ref=ref,
            send_sem=ring_send.at[kind],
            recv_sem=ring_recv.at[kind, zz, yy, max(side - 2, 0)],
            device_id=(x, to * ny + y, t),
            device_id_type=MESH,
        )

    def ring_own(kind, buffer):
        ring_copy(kind, buffer, z, y, right, 0).start()
        ring_copy(kind, buffer, z, y, left, 1).start()

    def ring_first(kind, buffer):
        def one(i, carry):
            yy = (y + i) % ny
            wait_bytes(buffer.at[z, yy], ring_recv.at[kind, z, yy, 0])
            ring_copy(kind, buffer, z, yy, right, 0).start()
            ring_copy(kind, buffer, z, yy, left, 1).start()
            return carry

        lax.fori_loop(1, ny, one, 0)

    def ring_step(kind, buffer, k, beside=None):
        def one(i, carry):
            yy = (y + i) % ny
            for side, zz, to in ((0, (z + nz - k) % nz, right), (1, (z + k) % nz, left)):
                if k <= full:
                    wait_bytes(buffer.at[zz, yy], ring_recv.at[kind, zz, yy, 0])
                    ring_copy(kind, buffer, zz, yy, to, side if k < full else side + 2).start()
                else:
                    wait_bytes(
                        buffer.at[zz, yy, pl.ds(side * (rank // 2), rank // 2)],
                        ring_recv.at[kind, zz, yy, side],
                    )
            if beside is not None:
                beside(i)
            return carry

        lax.fori_loop(0, ny, one, 0)

    slice_exchange(0, down_ref, downs)

    def send_rows(i, carry):
        px, py = peer(i)
        pltpu.make_async_remote_copy(
            src_ref=ids_own,
            dst_ref=ids_in.at[slot],
            send_sem=ids_send,
            recv_sem=ids_recv,
            device_id=(px, z * ny + py, t),
            device_id_type=MESH,
        ).start()
        pltpu.make_async_remote_copy(
            src_ref=hidden_ref.at[:, columns(px * ny + py)],
            dst_ref=rows_in.at[slot],
            send_sem=rows_send,
            recv_sem=rows_recv,
            device_id=(px, z * ny + py, t),
            device_id_type=MESH,
        ).start()
        return carry

    local[1].wait()
    ring_own(0, downs)
    each_peer(send_rows)
    slice_exchange(1, up_ref, ups)
    for copy in (local[3], local[4], local[5], local[6]):
        copy.start()
    ring_first(0, downs)

    local[4].wait()

    def unpack(i, carry):
        at = pl.ds(pl.multiple_of(i * EIGHT, EIGHT), EIGHT)
        wide = fresh[at].astype(jnp.float32)
        new_keys[at, :] = wide[:, 0, :]
        new_values[at, :] = wide[:, 1, :]
        return carry

    lax.fori_loop(0, rows // EIGHT, unpack, 0)
    ring_step(0, downs, 1)

    wait_bytes(ids_in.at[pl.ds(0, plane - 1)], ids_recv)
    spread = lax.broadcasted_iota(jnp.int32, (rows, blocks), 0) // block_rows == lax.broadcasted_iota(
        jnp.int32, (rows, blocks), 1
    )
    spread = jnp.where(spread, 1.0, 0.0).astype(jnp.bfloat16)

    def expand(s, carry):
        ids = lax.dot_general(spread, ids_in[s], NN, preferred_element_type=jnp.float32).astype(jnp.int32)
        at = pl.ds(pl.multiple_of(s * rows, rows), rows)
        key_rows[at, :] = ids // 2
        odd_rows[at, :] = ids % 2
        return carry

    lax.fori_loop(0, plane, expand, 0)
    local[0].wait()
    wait_bytes(rows_in.at[pl.ds(0, plane - 1)], rows_recv)

    per_chunk = ny * rank // LANES

    def use_down(i, chunks, first=False):
        lhs = rows_in[pl.ds(2 * i, 2)].reshape(2 * rows, part)
        at = pl.ds(pl.multiple_of(i * 2 * rows, 2 * rows), 2 * rows)
        named = key_rows[at, :]
        value = jnp.zeros((2 * rows, LANES), jnp.float32) if first else picked[at, :]
        for zz in chunks:
            product = lax.dot_general(
                lhs, downs[zz].reshape(ny * rank, part), NT, preferred_element_type=jnp.float32
            )
            for g in range(per_chunk):
                value = jnp.where(named == zz * per_chunk + g, product[:, g * LANES : (g + 1) * LANES], value)
        picked[at, :] = value

    def some_down(chunks, first=False):
        count = plane // 2 // ny

        def beside(i):
            for c in range(count):
                use_down(count * i + c, chunks, first)

        if plane // 2 % ny == 0:
            return beside, False
        return None, True

    def ring_and_down(k, chunks, first=False):
        beside, late = some_down(chunks, first)
        ring_step(0, downs, k, beside)
        if late:
            for i in range(plane // 2):
                use_down(i, chunks, first)

    near = [z, (z + nz - 1) % nz, (z + 1) % nz]
    for k in range(2, full + 1):
        ring_and_down(k, near if k == 2 else [(z + nz - k + 1) % nz, (z + k - 1) % nz], k == 2)
    local[2].wait()
    ring_own(1, ups)
    ring_first(1, ups)
    ring_and_down(full + 1, near if full == 1 else [(z + nz - full) % nz, (z + full) % nz], full == 1)

    def fold(u, carry):
        use_down(u, [(z + full + 1) % nz])
        upper = lax.broadcasted_iota(jnp.int32, (rows, LANES), 1) // rank
        both = []
        for h in range(2):
            at = pl.ds(pl.multiple_of((2 * u + h) * rows, rows), rows)
            kept = jnp.where(odd_rows[at, :] == upper, picked[at, :], 0.0)
            both.append(kept + pltpu.roll(kept, rank, 1))
        partial[pl.ds(pl.multiple_of(u * rows, rows), rows), :] = jnp.where(upper == 0, both[0], both[1])
        return carry

    lax.fori_loop(0, plane // 2, fold, 0)

    share = half_rows // nt

    def half_of(core):
        return pl.ds(pl.multiple_of(core * share, share), share)

    swap = pltpu.make_async_remote_copy(
        src_ref=partial.at[half_of(1 - t)],
        dst_ref=partner_in,
        send_sem=partner_send,
        recv_sem=partner_recv,
        device_id=(x, pool, 1 - t),
        device_id_type=MESH,
    )
    swap.start()
    swap.wait_recv()
    reduced[...] = partial[half_of(t), :] + partner_in[...]

    def packed(s):
        return pl.ds(pl.multiple_of(s * pack, pack), pack)

    def send_partial(i, carry):
        px, py = peer(i)
        pltpu.make_async_remote_copy(
            src_ref=reduced.at[packed(px * ny + py)],
            dst_ref=partial_in.at[slot],
            send_sem=partial_send,
            recv_sem=partial_recv,
            device_id=(px, z * ny + py, t),
            device_id_type=MESH,
        ).start()
        return carry

    each_peer(send_partial)
    partial_in[slot] = reduced[packed(slot), :]

    pairs = rows // (2 * EIGHT)
    request = lax.broadcasted_iota(jnp.int32, (1, EIGHT, LANES), 1)
    lane = lax.broadcasted_iota(jnp.int32, (1, EIGHT, LANES), 2)
    pair = request // 2
    mine = lane // slots == request % 2
    place = lane % slots
    fresh_lane = jnp.logical_and(jnp.logical_not(mine), place == request)
    pair_masks = [jnp.logical_and(mine, pair == j) for j in range(EIGHT // 2)]
    blank = jnp.zeros((slots - EIGHT, HEAD_SIZE), jnp.float32)

    def stacked(wide):
        return jnp.concatenate(wide, axis=0).astype(jnp.bfloat16)

    def fresh_tile(ref, at, h):
        new = ref[at, pl.ds(pl.multiple_of(h * HEAD_SIZE, HEAD_SIZE), HEAD_SIZE)]
        return jnp.concatenate([new, blank, new, blank], axis=0).astype(jnp.bfloat16)

    def chosen_scores(lhs, at, h):
        against = keys[at, h].reshape(EIGHT * slots, HEAD_SIZE)
        cached = lax.dot_general(lhs, against, NT, preferred_element_type=jnp.float32)
        new = lax.dot_general(lhs, fresh_tile(new_keys, at, h), NT, preferred_element_type=jnp.float32)
        chosen = new.reshape(group, EIGHT, LANES)
        for j in range(EIGHT // 2):
            tile = cached[:, j * LANES : (j + 1) * LANES].reshape(group, EIGHT, LANES)
            chosen = jnp.where(pair_masks[j], tile, chosen)
        return chosen * scale

    def base_scores(h, n):
        first = pl.multiple_of(n * 2 * EIGHT, 2 * EIGHT)
        wide = [
            queries[
                pl.ds(first, 2 * EIGHT),
                pl.ds(pl.multiple_of((h * group + g) * HEAD_SIZE, HEAD_SIZE), HEAD_SIZE),
            ].astype(jnp.float32)
            for g in range(group)
        ]
        for u in range(2):
            at = pl.ds(pl.multiple_of(first + u * EIGHT, EIGHT), EIGHT)
            lhs = stacked([w[u * EIGHT : (u + 1) * EIGHT] for w in wide])
            limit = jnp.zeros((1, EIGHT, LANES), jnp.int32)
            for i in range(EIGHT):
                limit = jnp.where(request == i, lengths_ref[first + u * EIGHT + i], limit)
            seen = jnp.logical_or(jnp.logical_and(mine, place < limit), fresh_lane)
            chosen = jnp.where(seen, chosen_scores(lhs, at, h), -1e30)
            scores_base[h, 2 * n + u] = chosen.reshape(tall, LANES)

    turns = (full + 1) * ny

    def beside_up(k):
        def beside(i):
            m = (k - 1) * ny + i
            if heads * pairs >= turns:
                base_scores(m // pairs, m % pairs)

        return beside

    local[3].wait()
    local[5].wait()
    ring_step(1, ups, 1, beside_up(1))
    wait_bytes(partial_in.at[pl.ds(0, plane - 1)], partial_recv)
    low = jnp.sum(partial_in[...], axis=0).astype(jnp.bfloat16)
    low_own[...] = low
    low_in[seat] = low

    def send_low_to(device):
        pltpu.make_async_remote_copy(
            src_ref=low_own,
            dst_ref=low_in.at[seat],
            send_sem=low_send,
            recv_sem=low_recv,
            device_id=device,
            device_id_type=MESH,
        ).start()

    def send_low(i, carry):
        px, py = peer(i)
        for pt in range(nt):
            send_low_to((px, z * ny + py, pt))
        return carry

    each_peer(send_low)
    send_low_to((x, pool, 1 - t))
    for k in range(2, full + 2):
        ring_step(1, ups, k, beside_up(k))
    for m in range(turns if heads * pairs >= turns else 0, heads * pairs):
        base_scores(m // pairs, m % pairs)
    wait_bytes(low_in.at[pl.ds(0, team - 1)], low_recv)

    groups = nz * ny * rank // LANES
    per = rows // pack

    def use_up(i, carry):
        px = (x + nx // 2 + i // (ny // 2)) % nx
        u = px * (ny // 2) + (y // 2 + 1 + i) % (ny // 2)
        low = low_in[pl.ds(u * per, per)].reshape(rows, LANES).astype(jnp.float32)
        turned = pltpu.roll(low, rank, 1)
        upper = lax.broadcasted_iota(jnp.int32, (rows, LANES), 1) // rank
        doubled = (jnp.where(upper == 0, low, turned), jnp.where(upper == 0, turned, low))
        lhs = []
        for h in range(2):
            at = pl.ds(pl.multiple_of((2 * u + h) * rows, rows), rows)
            kept = jnp.where(odd_rows[at, :] == upper, doubled[h], 0.0)
            named = key_rows[at, :]
            lhs.append(
                jnp.concatenate([jnp.where(named == g, kept, 0.0).astype(jnp.bfloat16) for g in range(groups)], axis=1)
            )
        change = lax.dot_general(
            jnp.concatenate(lhs, axis=0),
            ups[...].reshape(nz * ny * rank, part),
            NN,
            preferred_element_type=jnp.float32,
        ).astype(jnp.bfloat16)
        for h in range(2):
            s = 2 * u + h
            delta[s] = change[h * rows : (h + 1) * rows]

            @pl.when(s == slot)
            def _():
                delta_in[slot] = change[h * rows : (h + 1) * rows]

            @pl.when(s != slot)
            def _():
                pltpu.make_async_remote_copy(
                    src_ref=delta.at[s],
                    dst_ref=delta_in.at[slot],
                    send_sem=delta_send,
                    recv_sem=delta_recv.at[x],
                    device_id=(px, z * ny + s % ny, t),
                    device_id_type=MESH,
                ).start()

        return carry

    lax.fori_loop(0, plane // 2, use_up, 0)

    local[6].wait()
    per_part = part // HEAD_SIZE

    def head_columns(h):
        return pl.ds(pl.multiple_of(h * group * HEAD_SIZE, group * HEAD_SIZE), group * HEAD_SIZE)

    def attend(h, n):
        first = pl.multiple_of(n * 2 * EIGHT, 2 * EIGHT)
        wide = [
            delta_in[
                h * ny + g // per_part,
                pl.ds(first, 2 * EIGHT),
                g % per_part * HEAD_SIZE : (g % per_part + 1) * HEAD_SIZE,
            ].astype(jnp.float32)
            for g in range(group)
        ]
        outs = []
        for u in range(2):
            at = pl.ds(pl.multiple_of(first + u * EIGHT, EIGHT), EIGHT)
            lhs = stacked([w[u * EIGHT : (u + 1) * EIGHT] for w in wide])
            chosen = scores_base[h, 2 * n + u].reshape(group, EIGHT, LANES) + chosen_scores(lhs, at, h)
            raised = jnp.exp(chosen - jnp.max(chosen, axis=2, keepdims=True))
            total = jnp.sum(raised, axis=2, keepdims=True)
            cached = [jnp.where(m, raised, 0.0).reshape(tall, LANES) for m in pair_masks]
            new = jnp.where(mine, 0.0, raised).reshape(tall, LANES).astype(jnp.bfloat16)
            mixed = lax.dot_general(
                jnp.concatenate(cached, axis=1).astype(jnp.bfloat16),
                values[at, h].reshape(EIGHT * slots, HEAD_SIZE),
                NN,
                preferred_element_type=jnp.float32,
            ) + lax.dot_general(new, fresh_tile(new_values, at, h), NN, preferred_element_type=jnp.float32)
            outs.append((mixed.reshape(group, EIGHT, HEAD_SIZE) / total))
        for g in range(group):
            block = jnp.concatenate([o[g] for o in outs], axis=0)
            result[
                pl.ds(first, 2 * EIGHT), pl.ds(pl.multiple_of((h * group + g) * HEAD_SIZE, HEAD_SIZE), HEAD_SIZE)
            ] = block.astype(jnp.bfloat16)

    for j in range(nx):
        h = (x + nx - (nx // 2 + j) % nx) % nx
        arriving = ny - 1 if (nx // 2 + j) % nx == 0 else ny
        wait_bytes(delta_in.at[pl.ds(0, arriving)], delta_recv.at[h])

        def some(n, carry):
            attend(h, n)
            return carry

        lax.fori_loop(0, pairs, some, 0)
        pltpu.make_async_copy(result.at[:, head_columns(h)], out_ref.at[:, head_columns(h)], out_sem).start()

    wait_bytes(result, out_sem)
    wait_bytes(delta.at[pl.ds(0, plane - 1)], delta_send)
    wait_bytes(rows_in.at[pl.ds(0, plane - 1)], rows_send)
    wait_bytes(ids_in.at[pl.ds(0, plane - 1)], ids_send)
    swap.wait_send()
    wait_bytes(partial_in.at[pl.ds(0, plane - 1)], partial_send)
    wait_bytes(low_in.at[pl.ds(0, team - 1)], low_send)
    for kind, buffer in ((0, downs), (1, ups)):
        wait_bytes(buffer.at[0, pl.ds(0, ny - 1)], slice_send.at[kind])
        wait_bytes(buffer.at[pl.ds(0, 2 * full + 1)], ring_send.at[kind])


def body(
    sizes,
    hidden,
    query_base,
    new_kv,
    cache_keys,
    cache_values,
    lengths,
    adapter_ids,
    adapter_down,
    adapter_up,
):
    nx, ny, nz, nt = sizes
    plane = nx * ny
    team = plane * nt
    down = jnp.swapaxes(adapter_down, 1, 2)[0]
    up = adapter_up[0]
    rows, width = hidden.shape
    heads, slots = cache_keys.shape[1:3]
    rank = down.shape[0]
    part = width // plane
    blocks = adapter_ids.shape[0]
    total = plane * rows
    pack = total // 2 // team
    tall = width // (heads * HEAD_SIZE) * EIGHT
    bf16, f32, i32 = jnp.bfloat16, jnp.float32, jnp.int32
    dma = pltpu.SemaphoreType.DMA
    scalars = pl.BlockSpec(memory_space=pltpu.SMEM)
    anywhere = pl.BlockSpec(memory_space=pl.ANY)
    return pl.pallas_call(
        functools.partial(kernel, sizes),
        out_shape=jax.ShapeDtypeStruct((rows, width), bf16),
        in_specs=[scalars, scalars] + [anywhere] * 7,
        out_specs=anywhere,
        scratch_shapes=[
            pltpu.VMEM((plane, rows, part), bf16),
            pltpu.VMEM((blocks, LANES), bf16),
            pltpu.VMEM((plane, blocks, LANES), bf16),
            pltpu.VMEM((nz, ny, rank, part), bf16),
            pltpu.VMEM((nz, ny, rank, part), bf16),
            pltpu.VMEM((total, LANES), f32),
            pltpu.VMEM((total, LANES), i32),
            pltpu.VMEM((total, LANES), i32),
            pltpu.VMEM((total // 2, LANES), f32),
            pltpu.VMEM((total // 2 // nt, LANES), f32),
            pltpu.VMEM((total // 2 // nt, LANES), f32),
            pltpu.VMEM((plane, pack, LANES), f32),
            pltpu.VMEM((pack, LANES), bf16),
            pltpu.VMEM((team, pack, LANES), bf16),
            pltpu.VMEM((plane, rows, part), bf16),
            pltpu.VMEM((plane, rows, part), bf16),
            pltpu.VMEM((rows, width), bf16),
            pltpu.VMEM(new_kv.shape, bf16),
            pltpu.VMEM((rows, heads * HEAD_SIZE), f32),
            pltpu.VMEM((rows, heads * HEAD_SIZE), f32),
            pltpu.VMEM(cache_keys.shape, bf16),
            pltpu.VMEM(cache_values.shape, bf16),
            pltpu.VMEM((heads, rows // EIGHT, tall, LANES), f32),
            pltpu.VMEM((rows, width), bf16),
            dma((7,)),
            dma,
            dma,
            dma,
            dma,
            dma,
            dma((2,)),
            dma((2,)),
            dma((2, nz, ny, 2)),
            dma,
            dma,
            dma,
            dma,
            dma,
            dma,
            dma,
            dma((nx,)),
        ],
        compiler_params=pltpu.CompilerParams(
            collective_id=0, has_side_effects=True, vmem_limit_bytes=VMEM_LIMIT
        ),
    )(adapter_ids[:, 0], lengths, hidden, query_base, new_kv, cache_keys, cache_values, down, up)


def solution(mesh):
    in_specs = (
        P(("batch", "pool"), "tensor"),
        P(("batch", "pool"), "tensor"),
        P(("batch", "pool"), None, "tensor"),
        P(("batch", "pool"), "tensor", None, None),
        P(("batch", "pool"), "tensor", None, None),
        P(("batch", "pool")),
        P(("batch", "pool"), None),
        P("pool", "tensor", None),
        P("pool", None, "tensor"),
    )
    out_specs = P(("batch", "pool"), "tensor")
    pool = mesh.shape["pool"]
    sizes = (mesh.shape["batch"], CHIPS_Y, pool // CHIPS_Y, mesh.shape["tensor"])
    return jax.shard_map(
        functools.partial(body, sizes), mesh=mesh, in_specs=in_specs, out_specs=out_specs, check_vma=False
    )
```

time: 81.9 us -> 73.9 us (0.902); the launches traced: 80.9 us -> 73.8 us
  Pallas kernels: 79.4 us -> 71.9 us
    pallas_call x2 -> x1, Pallas kernels: 79.4 us -> 71.9 us  [body(): pl.pallas_call(functools.partial(kernel, sizes), out_shape=jax.ShapeDtype...]
where the time goes in v2:
time: 73.9 us; the launch traced here: 73.8 us
  Pallas kernels  71.9 us (97%)
  local copies, waits for them, and re-layouts  1.87 us (3%)
    pallas_call x1, Pallas kernels, body(): pl.pallas_call(functools.partial(kernel, sizes), out_shape=jax.ShapeDtype...  71.9 us
    unnamed x1, local copies, waits for them, and re-layouts  1.87 us

profile of v2, /device:TPU:8, one launch (start us, length us, event | category | flops | bytes accessed | tf_op | source)
XLA Modules:
  0.0 73.8 jit_solution(390015995749650063)
XLA Ops:
  0.0 71.9 %shard_map.91 = bf16[64,4096]{1,0:T(8,128)(2,1)} custom-call(s32[16]{0:T(128)} %bitcast.7, s32[64]{0:T(128)} %lengths_ref.1, bf16[64,4096]{1,0:T(8,128)(2,1)} %hidden_ref.1, bf16[64,4096]{1,0:T(8,128)(2,1)} %base_ref.1, bf16[64,2,512]{2,1,0:T(2,128)(2,1)} %fresh_ref.1, bf16[64,4,64,128]{3,2,1,0:T(8,128)(2,1)} %keys_ref.1, ...), custom_call_target="tpu_custom_call" | custom-call | tf_op jit(solution)/shard_map/pallas_call | solution.py:588
  71.9 1.9 %copy.11 = bf16[64,4096]{1,0:T(8,128)(2,1)} copy(bf16[64,4096]{1,0:T(8,128)(2,1)} %shard_map.91) | data formatting | bytes 1048576
